TPU v7x, 512 devices: a whole 4x4x16 slice. The times are simulated.
512 devices in a mesh: ctx: 64 (over y, z), head: 8 (over x, core).
Axes of the slice: x: 4, y: 4, z: 16, core: 2. Of those that a mesh axis runs over, the one named last changes fastest.
Arguments:
- queries: bfloat16 [16384, 4096], P('ctx', 'head'), may hold values from -200 to 200
- span_keys: bfloat16 [16384, 4096], P('ctx', 'head'), may hold values from -6 to 6
- span_values: bfloat16 [16384, 4096], P('ctx', 'head'), may hold values from -96 to 96
- cache_keys: bfloat16 [65536, 4096], P('ctx', 'head'), may hold values from -6 to 6
- cache_values: bfloat16 [65536, 4096], P('ctx', 'head'), may hold values from -96 to 96
- land_keys: bfloat16 [1024, 4096], P('ctx', 'head'), may hold values from -4.5 to 4.5
- land_values: bfloat16 [1024, 4096], P('ctx', 'head'), may hold values from -96 to 96
- out_weight: bfloat16 [4096, 4096], P('head', 'ctx'), may hold values from -0.09375 to 0.09375
- selection: int32 [256, 32, 4], P('ctx', 'head'), may hold values from 0 to 1023, as said below
Outputs:
- projected: bfloat16 [16384, 4096], P('ctx', 'head')
Inputs may be any that keep to these rules, and one draw needn't show every extreme that they name: `selection`: the 4 blocks of one query group and head are distinct. Count block b as owned by ctx index b // 16. Over all groups and heads of one device (one index of ctx and one of head), the selections within one owner's blocks number at most 4 and form at most 1 distinct pairs of block and head; some owner receives exactly that many of both from every device.
All inputs are finite; a program needn't handle non-finite values.
Results may differ from a plain program's by a relative error of at most 0.015.
Values may be sent and summed in bfloat16 or wider, within the bound.
A program may use at most 64 MiB of HBM per device.

v0:
```python
import math
import jax
import jax.numpy as jnp
from jax import lax
from jax.sharding import Mesh
from jax.sharding import PartitionSpec as P

BLOCK = 64
CTX = ("ctx_0", "ctx_1")


def in_one_piece(arrays, axis, dim, along):
    ends, at = ([], 0)
    for a in arrays[:-1]:
        at += a.shape[along]
        ends.append(at)
    both = jnp.concatenate(arrays, axis=along)
    return tuple(jnp.split(lax.all_gather(both, axis, axis=dim, tiled=True), ends, axis=along))


def cut_along(array, dim, peers):
    before, after = (array.shape[:dim], array.shape[dim + 1 :])
    return jnp.moveaxis(array.reshape(*before, peers, -1, *after), dim, 0)


def joined_along(tiles, dim):
    shape = list(tiles.shape[1:])
    shape[dim] *= tiles.shape[0]
    return jnp.moveaxis(tiles, 0, dim).reshape(shape)


def turned_blocks(tiles, axes, turns):
    shape = [lax.axis_size(a) for a in axes]
    tiles = tiles.reshape(*shape, *tiles.shape[1:])
    for k in turns:
        tiles = lax.all_to_all(tiles, axes[k], split_axis=k, concat_axis=k, tiled=True)
    return tiles.reshape(-1, *tiles.shape[len(axes) :])


def stepwise_exchange(array, axes, turns, split_dim, concat_dim):
    tiles = cut_along(array, split_dim, lax.axis_size(axes))
    return joined_along(turned_blocks(tiles, axes, turns), concat_dim)


def gather_in_order(array, axes, turns):
    tiles = array[None]
    for k in turns:
        tiles = lax.all_gather(tiles, axes[k], axis=0, tiled=True)
    current = [lax.axis_size(axes[k]) for k in reversed(turns)]
    tiles = tiles.reshape(*current, *array.shape)
    turned = sorted(range(len(turns)), key=lambda place: turns[len(turns) - 1 - place])
    return tiles.transpose(*turned, *range(len(turns), tiles.ndim)).reshape(-1, *array.shape)


def gathered_by_axis(array, axes, turns, dim):
    return joined_along(gather_in_order(array, axes, turns), dim)


def sum_at_owner(array, axis, dim):
    peers = lax.axis_size(axis)
    tiles = lax.all_to_all(cut_along(array, dim, peers), axis, 0, 0, tiled=True)
    return jnp.sum(tiles.astype(jnp.float32), axis=0)


def local(
    queries,
    span_keys,
    span_values,
    cache_keys,
    cache_values,
    land_keys,
    land_values,
    out_weight,
    selection,
):
    query_rows, row_width = queries.shape
    groups, head_dev, pick_count = selection.shape
    head_size = row_width // head_dev
    blocks_dev = cache_keys.shape[0] // BLOCK
    devices = lax.axis_size(CTX)
    scaling = 1.0 / math.sqrt(head_size)
    query_heads = queries.reshape(query_rows, head_dev, head_size)
    pieces = in_one_piece((land_keys, land_values), CTX, 0, 1)
    run_max = jnp.full((head_dev, query_rows), -jnp.inf, jnp.float32)
    run_sum = jnp.zeros((head_dev, query_rows), jnp.float32)
    run_acc = jnp.zeros((head_dev, query_rows, head_size), jnp.float32)
    key_piece = pieces[0].reshape(-1, head_dev, head_size)
    value_piece = pieces[1].reshape(-1, head_dev, head_size)
    scores = (
        jnp.einsum("qhd,nhd->hqn", query_heads, key_piece, preferred_element_type=jnp.float32)
        * scaling
    )
    new_max = jnp.max(scores, axis=2)
    weights = jnp.exp(scores - new_max[:, :, None])
    factor = jnp.exp(run_max - new_max)
    new_sum = run_sum * factor + jnp.sum(weights, axis=2)
    new_acc = run_acc * factor[:, :, None] + jnp.einsum(
        "hqn,nhd->hqd",
        weights.astype(jnp.bfloat16),
        value_piece,
        preferred_element_type=jnp.float32,
    )
    request_count = groups * head_dev * pick_count
    owners_flat = (selection // blocks_dev).reshape(request_count)
    block_flat = (selection % blocks_dev).reshape(request_count)
    head_flat = jnp.broadcast_to(
        jnp.arange(head_dev, dtype=jnp.int32)[None, :, None], selection.shape
    ).reshape(request_count)
    request_order = jnp.arange(request_count)
    earlier = request_order[None, :] < request_order[:, None]
    same_owner = owners_flat[:, None] == owners_flat[None, :]
    distinct_most = (head_dev * 2 * pick_count + devices - 1) // devices
    key_blocks = cache_keys.reshape(blocks_dev, BLOCK, head_dev, head_size)
    value_blocks = cache_values.reshape(blocks_dev, BLOCK, head_dev, head_size)
    asked_pairs = jnp.stack([block_flat, head_flat], axis=1)
    pair_ids = selection.reshape(request_count) * head_dev + head_flat
    same_pair = pair_ids[:, None] == pair_ids[None, :]
    is_first = jnp.logical_not(jnp.any(same_pair & earlier, axis=1))
    first_rank = jnp.sum(same_owner & earlier & is_first[None, :], axis=1)
    slot_ids = jnp.sum(jnp.where(same_pair & is_first[None, :], first_rank[None, :], 0), axis=1)
    wanted = (
        jnp.zeros((devices, distinct_most, 2), jnp.int32).at[owners_flat, slot_ids].set(asked_pairs)
    )
    asked_for = stepwise_exchange(wanted, CTX, (0, 1), 0, 0)
    sent_keys = key_blocks[asked_for[:, :, 0], :, asked_for[:, :, 1], :]
    sent_values = value_blocks[asked_for[:, :, 0], :, asked_for[:, :, 1], :]
    fetched_keys = lax.all_to_all(sent_keys, CTX, split_axis=0, concat_axis=0, tiled=True)
    fetched_values = lax.all_to_all(sent_values, CTX, split_axis=0, concat_axis=0, tiled=True)
    owner_grid = owners_flat.reshape(selection.shape)
    slot_grid = slot_ids.reshape(selection.shape)
    chosen_keys = fetched_keys[owner_grid, slot_grid]
    chosen_values = fetched_values[owner_grid, slot_grid].reshape(
        groups, head_dev, pick_count * BLOCK, head_size
    )
    query_groups = query_heads.reshape(groups, BLOCK, head_dev, head_size)
    chosen_scores = (
        jnp.einsum(
            "gqhd,ghpkd->ghqpk", query_groups, chosen_keys, preferred_element_type=jnp.float32
        )
        * scaling
    )
    chosen_scores = chosen_scores.reshape(groups, head_dev, BLOCK, pick_count * BLOCK)
    local_keys = span_keys.reshape(groups, BLOCK, head_dev, head_size)
    local_values = span_values.reshape(groups, BLOCK, head_dev, head_size)
    causal = jnp.arange(BLOCK)[:, None] >= jnp.arange(BLOCK)[None, :]
    local_scores = (
        jnp.einsum("gqhd,gkhd->ghqk", query_groups, local_keys, preferred_element_type=jnp.float32)
        * scaling
    )
    local_scores = jnp.where(causal[None, None], local_scores, -jnp.inf)
    land_top = jnp.transpose(new_max.reshape(head_dev, groups, BLOCK), (1, 0, 2))
    land_total = jnp.transpose(new_sum.reshape(head_dev, groups, BLOCK), (1, 0, 2))
    land_part = jnp.transpose(new_acc.reshape(head_dev, groups, BLOCK, head_size), (1, 0, 2, 3))
    overall_top = jnp.maximum(
        jnp.maximum(land_top, jnp.max(chosen_scores, axis=3)), jnp.max(local_scores, axis=3)
    )
    land_weight = jnp.exp(land_top - overall_top)
    chosen_weights = jnp.exp(chosen_scores - overall_top[..., None])
    local_weights = jnp.exp(local_scores - overall_top[..., None])
    denominator = (
        land_total * land_weight + jnp.sum(chosen_weights, axis=3) + jnp.sum(local_weights, axis=3)
    )
    numerator = land_part * land_weight[..., None]
    numerator = numerator + jnp.einsum(
        "ghqn,ghnd->ghqd",
        chosen_weights.astype(jnp.bfloat16),
        chosen_values,
        preferred_element_type=jnp.float32,
    )
    numerator = numerator + jnp.einsum(
        "ghqk,gkhd->ghqd",
        local_weights.astype(jnp.bfloat16),
        local_values,
        preferred_element_type=jnp.float32,
    )
    attended = (numerator / denominator[..., None]).astype(jnp.bfloat16)
    attended = jnp.transpose(attended, (0, 2, 1, 3)).reshape(query_rows, row_width)
    partial_out = jnp.dot(
        attended, gathered_by_axis(out_weight, CTX, (0, 1), 1), preferred_element_type=jnp.float32
    )
    summed = sum_at_owner(partial_out.astype(jnp.bfloat16), "head", 1)
    return summed.astype(jnp.bfloat16)


def solution(mesh):
    torus = Mesh(mesh.devices.reshape(4, 16, mesh.shape["head"]), ("ctx_0", "ctx_1", "head"))
    in_specs = (
        P(CTX, "head"),
        P(CTX, "head"),
        P(CTX, "head"),
        P(CTX, "head"),
        P(CTX, "head"),
        P(CTX, "head"),
        P(CTX, "head"),
        P("head", CTX),
        P(CTX, "head", None),
    )
    out_specs = P(CTX, "head")
    return jax.shard_map(local, mesh=torus, in_specs=in_specs, out_specs=out_specs, check_vma=False)
```

profile of v0, /device:TPU:1, one launch (start us, length us, event | category | flops | bytes accessed | tf_op | source)
XLA Modules:
  0.0 299.0 jit_solution(17440961947433692486)
XLA Ops:
  10.7 8.9 %all_to_all.25 = s32[4,16,1,1,2]{1,4,3,2,0:T(2,128)S(1)} all-to-all(s32[4,16,1,1,2]{1,4,3,2,0:T(2,128)S(1)} %copy.167), channel_id=1, replica_groups=mesh['ctx_0'=4,'ctx_1'=16,'head'=8] {'ctx_0'}, dimensions={0} | all-to-all | bytes 1024 | tf_op jit(solution)/shard_map/all_to_all | solution.py:36
  20.3 14.9 %all-to-all-start.1 = ((s32[4,16,1,1,2]{0,4,3,2,1:T(2,128)}), s32[4,16,1,1,2]{0,4,3,2,1:T(2,128)S(1)}, u32[]{:S(2)}, u32[]{:S(2)}) async-start(s32[4,16,1,1,2]{0,4,3,2,1:T(2,128)} %copy.168), calls=%async_computation.1 | async-start | bytes 32768 | tf_op jit(solution)/shard_map/all_to_all | solution.py:36
  36.9 9.7 %all-to-all-done.1 = s32[4,16,1,1,2]{0,4,3,2,1:T(2,128)S(1)} async-done(((s32[4,16,1,1,2]{0,4,3,2,1:T(2,128)}), s32[4,16,1,1,2]{0,4,3,2,1:T(2,128)S(1)}, u32[]{:S(2)}, u32[]{:S(2)}) %all-to-all-start.1) | async-done | bytes 544 | tf_op jit(solution)/shard_map/all_to_all | solution.py:36
  46.8 1.7 gather_fusion
  48.6 4.7 %all-to-all-start.2 = ((bf16[64,1,64,128]{3,2,1,0:T(8,128)(2,1)}), bf16[64,1,64,128]{3,2,1,0:T(8,128)(2,1)S(1)}, u32[]{:S(2)}, u32[]{:S(2)}) async-start(bf16[64,1,64,128]{3,2,1,0:T(8,128)(2,1)} %bitcast.12), calls=%async_computation.2 | async-start | bytes 2097152 | tf_op jit(solution)/shard_map/all_to_all | solution.py:127
  53.3 10.7 %all-gather = bf16[2048,64]{0,1:T(8,128)(2,1)S(1)} all-gather(bf16[512,64]{0,1:T(8,128)(2,1)S(1)} %copy-done.5), channel_id=2, replica_groups=mesh['ctx_0'=4,'ctx_1'=16,'head'=8] {'ctx_0'}, dimensions={0}, use_global_device_ids=true | all-gather | bytes 327680 | tf_op jit(solution)/shard_map/all_gather | solution.py:48
  65.3 1.8 gather_fusion.2
  67.1 35.5 %all-to-all-done.2 = bf16[64,1,64,128]{3,2,1,0:T(8,128)(2,1)S(1)} async-done(((bf16[64,1,64,128]{3,2,1,0:T(8,128)(2,1)}), bf16[64,1,64,128]{3,2,1,0:T(8,128)(2,1)S(1)}, u32[]{:S(2)}, u32[]{:S(2)}) %all-to-all-start.2) | async-done | bytes 1048608 | tf_op jit(solution)/shard_map/all_to_all | solution.py:127
  102.6 11.2 %all-to-all-start.3 = ((bf16[64,1,64,128]{3,2,1,0:T(8,128)(2,1)}), bf16[64,1,64,128]{3,2,1,0:T(8,128)(2,1)S(1)}, u32[]{:S(2)}, u32[]{:S(2)}) async-start(bf16[64,1,64,128]{3,2,1,0:T(8,128)(2,1)} %bitcast.22), calls=%async_computation.3 | async-start | bytes 2097152 | tf_op jit(solution)/shard_map/all_to_all | solution.py:128
  115.3 1.7 reshape.210
  118.1 56.2 %all-gather.4.cloned.1.call-done = bf16[1024,1024]{1,0:T(8,128)(2,1)} async-done(((bf16[16,1024]{1,0:T(8,128)(2,1)}), bf16[1024,1024]{1,0:T(8,128)(2,1)}) %all-gather.4.cloned.1.call-update) | async-done | bytes 2097168 | tf_op jit(solution)/shard_map/all_gather | solution.py:18
  174.3 2.7 fusion.49
  177.0 2.3 copy.196
  179.2 4.0 %bitcast_reduce_fusion = (f32[4,256]{1,0:T(4,128)S(1)}, f32[4,1024,256]{2,1,0:T(8,128)}) fusion(bf16[1024,4,128]{0,2,1:T(8,128)(2,1)} %bitcast.142, bf16[256,512]{1,0:T(8,128)(2,1)S(1)} %copy-done), kind=kOutput, calls=%fused_computation.7 | convolution fusion | flops 270531584 | bytes 5509120 | tf_op jit(solution)/shard_map/qhd,nhd->hqn/dot_general | solution.py:90
  183.3 2.9 fusion.1
  187.5 4.4 %fusion.11 = f32[4,256,128]{2,1,0:T(8,128)} fusion(bf16[1024,4,128]{0,2,1:T(8,128)(2,1)} %bitcast.141, f32[4,1024,256]{2,1,0:T(8,128)} %get-tuple-element.19, f32[4,256]{1,0:T(4,128)S(1)} %get-tuple-element.18, f32[4,256]{1,0:T(4,128)S(1)} %exponential_multiply_fusion), kind=kOutput, calls=%fused_computation.24 | convolution fusion | flops 271712256 | bytes 5775360 | tf_op jit(solution)/shard_map/hqn,nhd->hqd/dot_general | solution.py:97
  191.9 1.7 gather_fusion.1
  193.6 1.7 bitcast_reduce_fusion.1
  195.3 1.6 copy.176
  196.8 1.7 gather_fusion.3
  201.5 2.2 fusion.16
  203.9 42.9 %all-gather.6.cloned.1.call-done = bf16[64,512,64]{1,2,0:T(8,128)(2,1)} async-done(((bf16[4,512,64]{1,2,0:T(8,128)(2,1)}), bf16[64,512,64]{1,2,0:T(8,128)(2,1)}) %all-gather.6.cloned.1.call-update) | async-done | bytes 4194320 | tf_op jit(solution)/shard_map/all_gather | solution.py:48
  246.8 2.7 copy.185
  251.0 40.1 %all_to_all.26 = bf16[8,256,512]{2,1,0:T(8,128)(2,1)S(1)} all-to-all(bf16[8,256,512]{2,1,0:T(8,128)(2,1)S(1)} %bitcast.138), channel_id=1, replica_groups=mesh['ctx_0'=4,'ctx_1'=16,'head'=8] {'head'}, dimensions={0} | all-to-all | bytes 4194304 | tf_op jit(solution)/shard_map/all_to_all | solution.py:61
  (65 shorter events, 17.5 us)
Async XLA Ops:
  6.5 167.7 %all-gather.4.cloned.1.call-start = ((), (), s32[]{:S(2)}) async-start(), calls=%async_computation.5 | async-start | bytes 2129920 | tf_op jit(solution)/shard_map/all_gather | solution.py:18
  20.3 26.3 %all-to-all-start.1 = ((s32[4,16,1,1,2]{0,4,3,2,1:T(2,128)}), s32[4,16,1,1,2]{0,4,3,2,1:T(2,128)S(1)}, u32[]{:S(2)}, u32[]{:S(2)}) async-start(s32[4,16,1,1,2]{0,4,3,2,1:T(2,128)} %copy.168), calls=%async_computation.1 | async-start | bytes 32768 | tf_op jit(solution)/shard_map/all_to_all | solution.py:36
  35.2 18.1 %copy-start.5 = (bf16[512,64]{0,1:T(8,128)(2,1)S(1)}, bf16[512,64]{0,1:T(8,128)(2,1)}, u32[]{:S(2)}) copy-start(bf16[512,64]{0,1:T(8,128)(2,1)} %param.16) | copy-start | bytes 196612
  36.9 27.8 %copy-start.2 = (bf16[1024,512]{1,0:T(8,128)(2,1)S(1)}, bf16[1024,512]{1,0:T(8,128)(2,1)}, u32[]{:S(2)}) copy-start(bf16[1024,512]{1,0:T(8,128)(2,1)} %param.13) | copy-start | bytes 3145732
  48.6 54.0 %all-to-all-start.2 = ((bf16[64,1,64,128]{3,2,1,0:T(8,128)(2,1)}), bf16[64,1,64,128]{3,2,1,0:T(8,128)(2,1)S(1)}, u32[]{:S(2)}, u32[]{:S(2)}) async-start(bf16[64,1,64,128]{3,2,1,0:T(8,128)(2,1)} %bitcast.12), calls=%async_computation.2 | async-start | bytes 2097152 | tf_op jit(solution)/shard_map/all_to_all | solution.py:127
  53.2 193.6 %all-gather.6.cloned.1.call-start = ((), (), s32[]{:S(2)}) async-start(), calls=%async_computation.6 | async-start | bytes 4456448 | tf_op jit(solution)/shard_map/all_gather | solution.py:48
  64.7 49.3 %copy-start = (bf16[256,512]{1,0:T(8,128)(2,1)S(1)}, bf16[256,512]{1,0:T(8,128)(2,1)}, u32[]{:S(2)}) copy-start(bf16[256,512]{1,0:T(8,128)(2,1)} %param.9) | copy-start | bytes 786436
  102.6 94.3 %all-to-all-start.3 = ((bf16[64,1,64,128]{3,2,1,0:T(8,128)(2,1)}), bf16[64,1,64,128]{3,2,1,0:T(8,128)(2,1)S(1)}, u32[]{:S(2)}, u32[]{:S(2)}) async-start(bf16[64,1,64,128]{3,2,1,0:T(8,128)(2,1)} %bitcast.22), calls=%async_computation.3 | async-start | bytes 2097152 | tf_op jit(solution)/shard_map/all_to_all | solution.py:128
  114.1 4.0 %copy-start.3 = (bf16[4,64,4,128]{3,2,1,0:T(4,128)(2,1)}, bf16[4,64,4,128]{3,2,1,0:T(4,128)(2,1)S(1)}, u32[]{:S(2)}) copy-start(bf16[4,64,4,128]{3,2,1,0:T(4,128)(2,1)S(1)} %reshape_reshape.11) | copy-start | bytes 786436
  187.5 6.1 %copy-start.4 = (bf16[4,64,4,128]{3,2,1,0:T(4,128)(2,1)S(1)}, bf16[4,64,4,128]{3,2,1,0:T(4,128)(2,1)}, u32[]{:S(2)}) copy-start(bf16[4,64,4,128]{3,2,1,0:T(4,128)(2,1)} %copy-done.3) | copy-start | bytes 786436
  195.3 4.9 %copy-start.1 = (bf16[4,64,4,128]{3,2,1,0:T(4,128)(2,1)S(1)}, bf16[4,64,4,128]{3,2,1,0:T(4,128)(2,1)}, u32[]{:S(2)}) copy-start(bf16[4,64,4,128]{3,2,1,0:T(4,128)(2,1)} %reshape.210) | copy-start | bytes 786436
Sparse Core Ops, SparseCore 0:
  10.3 163.9 all-gather.3
  176.4 70.4 all-gather.5
where the time goes:
time: 300 us; the launch traced here: 299 us
  waiting for transfers between devices  144 us (48%)
  blocking collectives  59.7 us (20%)
  starting transfers between devices  30.9 us (10%)
  local copies, waits for them, and re-layouts  26.3 us (9%)
  matrix products  15.9 us (5%)
  between operations  13.7 us (5%)
  other arithmetic  8.18 us (3%)
    all_gather x1, waiting for transfers between devices, in_one_piece(): lax.all_gather(both, axis, axis=dim, tiled=True)  56.2 us
    all_gather x1, waiting for transfers between devices, gather_in_order(): tiles = lax.all_gather(tiles, axes[k], axis=0, tiled=True)  42.9 us
    all_to_all x1, blocking collectives, sum_at_owner(): tiles = lax.all_to_all(cut_along(array, dim, peers), axis, 0, 0, tiled=True)  40.1 us
    all_to_all x1, waiting for transfers between devices, local(): lax.all_to_all(sent_keys, CTX, split_axis=0, concat_axis=0, tiled=True)  35.5 us
    all_to_all x1, starting transfers between devices, turned_blocks(): lax.all_to_all(tiles, axes[k], split_axis=k, concat_axis=k, tiled=True)  14.9 us
    all_to_all x1, starting transfers between devices, local(): lax.all_to_all(sent_values, CTX, split_axis=0, concat_axis=0, tiled=True)  11.2 us
    all_gather x1, blocking collectives, gather_in_order(): tiles = lax.all_gather(tiles, axes[k], axis=0, tiled=True)  10.7 us
    all_to_all x1, waiting for transfers between devices, turned_blocks(): lax.all_to_all(tiles, axes[k], split_axis=k, concat_axis=k, tiled=True)  9.71 us
  transfers between devices with their start and end apart: 5, of which 4 were waited for; matrix products, arithmetic and copies ran while one was open for 15% of the time, Pallas kernels for 0%

commit v1 on v0

--- a/solution.py
+++ b/solution.py
@@ -4,6 +4,7 @@
 from jax import lax
 from jax.sharding import Mesh
 from jax.sharding import PartitionSpec as P
+from jax.lax import all_to_all, axis_size
 
 BLOCK = 64
 CTX = ("ctx_0", "ctx_1")
@@ -45,7 +46,15 @@
 def gather_in_order(array, axes, turns):
     tiles = array[None]
     for k in turns:
-        tiles = lax.all_gather(tiles, axes[k], axis=0, tiled=True)
+
+        def supply_all_targets_on(original, device_axis, dimension_no):
+            answer = axis_size(device_axis)
+            lower = jnp.stack(answer * [original], axis=0)
+            v_next = all_to_all(lower, device_axis, 0, 0)
+            tmp = jnp.concatenate(v_next, dimension_no)
+            return tmp
+
+        tiles = supply_all_targets_on(tiles, axes[k], 0)
     current = [lax.axis_size(axes[k]) for k in reversed(turns)]
     tiles = tiles.reshape(*current, *array.shape)
     turned = sorted(range(len(turns)), key=lambda place: turns[len(turns) - 1 - place])

time: 300 us -> 464 us (1.55)
  waiting for transfers between devices: 144 us -> 261 us
  blocking collectives: 59.7 us -> 103 us
    all_gather x1, waiting for transfers between devices: 56.2 us -> 203 us  [in_one_piece(): lax.all_gather(both, axis, axis=dim, tiled=True)]
    all_to_all x0 -> x1, blocking collectives: none -> 59.1 us  [local(): lax.all_to_all(sent_values, CTX, split_axis=0, concat_axis=0, tiled=True)]
    all_gather x1 -> x0, waiting for transfers between devices: 42.9 us -> none  [gather_in_order(): tiles = lax.all_gather(tiles, axes[k], axis=0, tiled=True)]
    all_gather x1 -> x0, blocking collectives: 10.7 us -> none  [gather_in_order(): tiles = lax.all_gather(tiles, axes[k], axis=0, tiled=True)]
    all_to_all x1, waiting for transfers between devices: 35.5 us -> 44.8 us  [local(): lax.all_to_all(sent_keys, CTX, split_axis=0, concat_axis=0, tiled=True)]
    all_to_all x1, blocking collectives: 40.1 us -> 34.7 us  [sum_at_owner(): tiles = lax.all_to_all(cut_along(array, dim, peers), axis, 0, 0, tiled=True)]
    all_to_all x1 -> x2, starting transfers between devices: 11.2 us -> 12.5 us  [supply_all_targets_on(): v_next = all_to_all(lower, device_axis, 0, 0)]
  transfers between devices with their start and end apart: 5 -> 5, of which waited for: 4 -> 4; matrix products, arithmetic and copies ran while one was open for 15% -> 9% of each run, Pallas kernels for 0% -> 0%
where the time goes in v1:
time: 464 us; the launch traced here: 462 us
  waiting for transfers between devices  261 us (56%)
  blocking collectives  103 us (22%)
  starting transfers between devices  32.3 us (7%)
  local copies, waits for them, and re-layouts  28.2 us (6%)
  matrix products  16.9 us (4%)
  between operations  13.7 us (3%)
  other arithmetic  7.46 us (2%)
    all_gather x1, waiting for transfers between devices, in_one_piece(): lax.all_gather(both, axis, axis=dim, tiled=True)  203 us
    all_to_all x1, blocking collectives, local(): lax.all_to_all(sent_values, CTX, split_axis=0, concat_axis=0, tiled=True)  59.1 us
    all_to_all x1, waiting for transfers between devices, local(): lax.all_to_all(sent_keys, CTX, split_axis=0, concat_axis=0, tiled=True)  44.8 us
    all_to_all x1, blocking collectives, sum_at_owner(): tiles = lax.all_to_all(cut_along(array, dim, peers), axis, 0, 0, tiled=True)  34.7 us
    all_to_all x1, starting transfers between devices, turned_blocks(): lax.all_to_all(tiles, axes[k], split_axis=k, concat_axis=k, tiled=True)  14.9 us
    all_to_all x2, starting transfers between devices, supply_all_targets_on(): v_next = all_to_all(lower, device_axis, 0, 0)  12.5 us
    all_to_all x1, waiting for transfers between devices, turned_blocks(): lax.all_to_all(tiles, axes[k], split_axis=k, concat_axis=k, tiled=True)  9.66 us
  transfers between devices with their start and end apart: 5, of which 4 were waited for; matrix products, arithmetic and copies ran while one was open for 9% of the time, Pallas kernels for 0%

profile of v1, /device:TPU:1, one launch (start us, length us, event | category | flops | bytes accessed | tf_op | source)
XLA Modules:
  0.0 461.9 jit_solution(18258083947513835523)
XLA Ops:
  9.3 8.9 %all_to_all.35 = s32[4,16,1,1,2]{1,4,3,2,0:T(2,128)S(1)} all-to-all(s32[4,16,1,1,2]{1,4,3,2,0:T(2,128)S(1)} %copy.138), channel_id=1, replica_groups=mesh['ctx_0'=4,'ctx_1'=16,'head'=8] {'ctx_0'}, dimensions={0} | all-to-all | bytes 1024 | tf_op jit(solution)/shard_map/all_to_all | solution.py:37
  19.0 14.9 %all-to-all-start.1 = ((s32[4,16,1,1,2]{0,4,3,2,1:T(2,128)}), s32[4,16,1,1,2]{0,4,3,2,1:T(2,128)S(1)}, u32[]{:S(2)}, u32[]{:S(2)}) async-start(s32[4,16,1,1,2]{0,4,3,2,1:T(2,128)} %copy.139), calls=%async_computation.1 | async-start | bytes 32768 | tf_op jit(solution)/shard_map/all_to_all | solution.py:37
  35.6 9.7 %all-to-all-done.1 = s32[4,16,1,1,2]{0,4,3,2,1:T(2,128)S(1)} async-done(((s32[4,16,1,1,2]{0,4,3,2,1:T(2,128)}), s32[4,16,1,1,2]{0,4,3,2,1:T(2,128)S(1)}, u32[]{:S(2)}, u32[]{:S(2)}) %all-to-all-start.1) | async-done | bytes 544 | tf_op jit(solution)/shard_map/all_to_all | solution.py:37
  46.0 3.4 all-to-all-start.4
  49.6 1.7 gather_fusion
  51.4 3.6 all-to-all-done.4
  54.9 4.7 %all-to-all-start.2 = ((bf16[64,1,64,128]{3,2,1,0:T(8,128)(2,1)}), bf16[64,1,64,128]{3,2,1,0:T(8,128)(2,1)S(1)}, u32[]{:S(2)}, u32[]{:S(2)}) async-start(bf16[64,1,64,128]{3,2,1,0:T(8,128)(2,1)} %bitcast.12), calls=%async_computation.2 | async-start | bytes 2097152 | tf_op jit(solution)/shard_map/all_to_all | solution.py:136
  61.0 44.8 %all-to-all-done.2 = bf16[64,1,64,128]{3,2,1,0:T(8,128)(2,1)S(1)} async-done(((bf16[64,1,64,128]{3,2,1,0:T(8,128)(2,1)}), bf16[64,1,64,128]{3,2,1,0:T(8,128)(2,1)S(1)}, u32[]{:S(2)}, u32[]{:S(2)}) %all-to-all-start.2) | async-done | bytes 1048608 | tf_op jit(solution)/shard_map/all_to_all | solution.py:136
  105.7 59.1 %all_to_all.36 = bf16[64,1,64,128]{3,2,1,0:T(8,128)(2,1)S(1)} all-to-all(bf16[64,1,64,128]{3,2,1,0:T(8,128)(2,1)S(1)} %bitcast.135), channel_id=1, replica_groups=mesh['ctx_0'=4,'ctx_1'=16,'head'=8] {'ctx_0','ctx_1'}, dimensions={0} | all-to-all | bytes 2097152 | tf_op jit(solution)/shard_map/all_to_all | solution.py:137
  164.8 2.5 stack.11
  167.3 9.1 %all-to-all-start.5 = ((bf16[16,4,512,64]{2,3,1,0:T(8,128)(2,1)}), bf16[16,4,512,64]{2,3,1,0:T(8,128)(2,1)}, u32[]{:S(2)}, u32[]{:S(2)}) async-start(bf16[16,4,512,64]{2,3,1,0:T(8,128)(2,1)} %stack.11), calls=%async_computation.5 | async-start | bytes 8388608 | tf_op jit(solution)/shard_map/all_to_all | solution.py:53
  179.4 2.0 fusion.50
  181.4 202.7 %all-gather.2.cloned.1.call-done = bf16[1024,1024]{1,0:T(8,128)(2,1)} async-done(((bf16[16,1024]{1,0:T(8,128)(2,1)}), bf16[1024,1024]{1,0:T(8,128)(2,1)}) %all-gather.2.cloned.1.call-update) | async-done | bytes 2097168 | tf_op jit(solution)/shard_map/all_gather | solution.py:19
  384.1 3.0 fusion.49
  387.1 2.3 copy.166
  389.3 4.0 bitcast_reduce_fusion
  393.4 2.9 fusion.1
  396.3 2.3 copy.167
  398.6 4.4 fusion.11
  403.0 1.8 gather_fusion.1
  408.0 1.8 gather_fusion.3
  412.7 2.2 fusion.16
  415.1 2.7 copy.155
  419.2 34.7 %all_to_all.37 = bf16[8,256,512]{2,1,0:T(8,128)(2,1)S(1)} all-to-all(bf16[8,256,512]{2,1,0:T(8,128)(2,1)S(1)} %bitcast.134), channel_id=1, replica_groups=mesh['ctx_0'=4,'ctx_1'=16,'head'=8] {'head'}, dimensions={0} | all-to-all | bytes 4194304 | tf_op jit(solution)/shard_map/all_to_all | solution.py:70
  (67 shorter events, 19.4 us)
Async XLA Ops:
  6.5 38.7 %copy-start.4 = (bf16[512,64]{0,1:T(8,128)(2,1)S(1)}, bf16[512,64]{0,1:T(8,128)(2,1)}, u32[]{:S(2)}) copy-start(bf16[512,64]{0,1:T(8,128)(2,1)} %param.16) | copy-start | bytes 196612
  19.0 26.3 %all-to-all-start.1 = ((s32[4,16,1,1,2]{0,4,3,2,1:T(2,128)}), s32[4,16,1,1,2]{0,4,3,2,1:T(2,128)S(1)}, u32[]{:S(2)}, u32[]{:S(2)}) async-start(s32[4,16,1,1,2]{0,4,3,2,1:T(2,128)} %copy.139), calls=%async_computation.1 | async-start | bytes 32768 | tf_op jit(solution)/shard_map/all_to_all | solution.py:37
  33.9 25.7 %copy-start.1 = (bf16[1024,512]{1,0:T(8,128)(2,1)S(1)}, bf16[1024,512]{1,0:T(8,128)(2,1)}, u32[]{:S(2)}) copy-start(bf16[1024,512]{1,0:T(8,128)(2,1)} %param.13) | copy-start | bytes 3145732
  46.0 8.9 %all-to-all-start.4 = ((bf16[4,1,512,64]{2,3,1,0:T(8,128)(2,1)}), bf16[4,1,512,64]{2,3,1,0:T(8,128)(2,1)S(1)}, u32[]{:S(2)}, u32[]{:S(2)}) async-start(bf16[4,1,512,64]{2,3,1,0:T(8,128)(2,1)} %stack.10), calls=%async_computation.4 | async-start | bytes 524288 | tf_op jit(solution)/shard_map/all_to_all | solution.py:53
  54.9 50.8 %all-to-all-start.2 = ((bf16[64,1,64,128]{3,2,1,0:T(8,128)(2,1)}), bf16[64,1,64,128]{3,2,1,0:T(8,128)(2,1)S(1)}, u32[]{:S(2)}, u32[]{:S(2)}) async-start(bf16[64,1,64,128]{3,2,1,0:T(8,128)(2,1)} %bitcast.12), calls=%async_computation.2 | async-start | bytes 2097152 | tf_op jit(solution)/shard_map/all_to_all | solution.py:136
  167.3 9.3 %copy-start.5 = (bf16[16,512]{1,0:T(8,128)(2,1)S(1)}, bf16[16,512]{1,0:T(8,128)(2,1)}, u32[]{:S(2)}) copy-start(bf16[16,512]{1,0:T(8,128)(2,1)} %param.15) | copy-start | bytes 49156
  167.3 9.3 %copy-start.6 = (bf16[16,512]{1,0:T(8,128)(2,1)S(1)}, bf16[16,512]{1,0:T(8,128)(2,1)}, u32[]{:S(2)}) copy-start(bf16[16,512]{1,0:T(8,128)(2,1)} %param.14) | copy-start | bytes 49156
  167.3 10.2 %copy-start = (bf16[256,512]{1,0:T(8,128)(2,1)S(1)}, bf16[256,512]{1,0:T(8,128)(2,1)}, u32[]{:S(2)}) copy-start(bf16[256,512]{1,0:T(8,128)(2,1)} %param.9) | copy-start | bytes 786436
  167.3 10.3 %copy-start.3 = (bf16[256,512]{1,0:T(8,128)(2,1)S(1)}, bf16[256,512]{1,0:T(8,128)(2,1)}, u32[]{:S(2)}) copy-start(bf16[256,512]{1,0:T(8,128)(2,1)} %param.10) | copy-start | bytes 786436
  167.3 247.8 %all-to-all-start.5 = ((bf16[16,4,512,64]{2,3,1,0:T(8,128)(2,1)}), bf16[16,4,512,64]{2,3,1,0:T(8,128)(2,1)}, u32[]{:S(2)}, u32[]{:S(2)}) async-start(bf16[16,4,512,64]{2,3,1,0:T(8,128)(2,1)} %stack.11), calls=%async_computation.5 | async-start | bytes 8388608 | tf_op jit(solution)/shard_map/all_to_all | solution.py:53
  176.4 207.7 %all-gather.2.cloned.1.call-start = ((), (), s32[]{:S(2)}) async-start(), calls=%async_computation.7 | async-start | bytes 2129920 | tf_op jit(solution)/shard_map/all_gather | solution.py:19
  177.5 211.8 %copy-start.2 = (bf16[4,64,4,128]{3,2,1,0:T(4,128)(2,1)}, bf16[4,64,4,128]{3,2,1,0:T(4,128)(2,1)S(1)}, u32[]{:S(2)}) copy-start(bf16[4,64,4,128]{3,2,1,0:T(4,128)(2,1)S(1)} %reshape_reshape.11) | copy-start | bytes 786436
Sparse Core Ops, SparseCore 0:
  180.1 203.8 all-gather.1
